TPU v7x, 32 devices: a whole 2x2x4 slice. The times are simulated.
32 devices in a mesh: narrow: 4 (over y, core), wide: 8 (over z, x).
Axes of the slice: x: 2, y: 2, z: 4, core: 2. Of those that a mesh axis runs over, the one named last changes fastest.
Arguments:
- inputs: bfloat16 [256, 8, 100], P('wide'), may hold values from -6 to 6
- cotangent: bfloat16 [256, 8, 10], P('wide'), may hold values from -6 to 6
- step_mask: int32 [256, 8], P('wide'), may hold values 0 or 1
- washout: int32 [256], P('wide'), may hold values from 0 to 1
- lengths: int32 [256], P('wide'), may hold values from 4 to 8
- leak_groups: int32 [2, 4, 2048], P(None, 'narrow'), may hold values 0 or 1
- leak_two: float32 [4], P('narrow'), may hold values from 0.03 to 0.3
- w_one: bfloat16 [4, 2048, 2048], P('narrow'), may hold values from -0.125 to 0.125
- v_one: bfloat16 [4, 100, 2048], P('narrow'), may hold values from -0.625 to 0.625
- v_two: bfloat16 [4, 2048, 2048], P('narrow'), may hold values from -0.25 to 0.25
- w_two: bfloat16 [4, 2048, 2048], P('narrow'), may hold values from -0.125 to 0.125
- w_out: bfloat16 [8192, 10], P('narrow'), may hold values from -0.0625 to 0.0625
- b_out: float32 [10], replicated, may hold values from -4 to 4
Outputs:
- output: float32 [256, 8, 10], P('wide', 'narrow')
- input_grad: float32 [256, 8, 100], P('wide')
- grad_w_one: float32 [4, 2048, 2048], P('narrow', None, 'wide')
- grad_v_one: float32 [4, 100, 2048], P('narrow', None, 'wide')
- grad_v_two: float32 [4, 2048, 2048], P('narrow', None, 'wide')
- grad_w_two: float32 [4, 2048, 2048], P('narrow', None, 'wide')
- grad_w_out: float32 [8192, 10], P('narrow')
- grad_b_out: float32 [10], replicated
All inputs are finite; a program needn't handle non-finite values. No bound on the sum of `step_mask` or of `leak_groups` on one device may be relied on, other than what follows from the above.
Results may differ from a plain program's by a relative error of at most 0.0055.
Values may be sent and summed in bfloat16 or wider, within the bound.
No kernel may reach another device: no remote copies, remote signals or barrier semaphores. Data moves between devices by JAX's collectives and lax.ppermute only.
A program may use at most 192 MiB of HBM per device.

v0:
```python
import jax
import jax.numpy as jnp
from jax import lax
from jax.sharding import PartitionSpec as P


def feature_grad(grads, values, valid, mean, inv, count, sum_g, sum_gx):
    slope = -0.5 * inv * inv * inv * (sum_gx - mean * sum_g)
    shift = -inv * sum_g - 2.0 * mean * slope
    result = inv * grads + valid[:, :, None] * (shift + 2.0 * values * slope) / count
    return result.astype(jnp.bfloat16)


def statistics(values, valid):
    weights = valid[:, :, None]
    return (
        jnp.sum(weights * values, axis=(0, 1)),
        jnp.sum(weights * values * values, axis=(0, 1)),
        jnp.sum(valid),
    )


def normalize(values, totals):
    mean = totals[0] / totals[2]
    inv = lax.rsqrt(totals[1] / totals[2] - mean * mean + 1e-05)
    return (mean, inv, ((values - mean) * inv).astype(jnp.bfloat16))


def back_layer(extra, pre, rate, weight):

    def back_step(carry, items):
        ext_now, pre_now = items
        grad_h = ext_now + carry
        slope = 1.0 - jnp.square(jnp.tanh(pre_now))
        grad_p = (grad_h * rate * slope).astype(jnp.bfloat16)
        carry = (1.0 - rate) * grad_h + lax.dot_general(
            grad_p, weight, (((1,), (1,)), ((), ())), preferred_element_type=jnp.float32
        )
        return (carry, grad_p)

    start = jnp.zeros(extra.shape[1:], jnp.float32)
    final, grad_pre = lax.scan(back_step, start, (extra, pre), reverse=True)
    return grad_pre


def shifted(states):
    return jnp.concatenate([jnp.zeros_like(states[:1]), states[:-1]], axis=0)


def outer_sum(left, right):
    return jnp.einsum("tbr,tbq->rq", left, right, preferred_element_type=jnp.float32)


def on_device(
    inputs,
    cotangent,
    step_mask,
    washout,
    lengths,
    leak_groups,
    leak_two,
    w_one,
    v_one,
    v_two,
    w_two,
    w_out,
    b_out,
):
    rates = jnp.where(leak_groups == 0, jnp.float32(0.3), leak_two[None, :, None])
    rate_one = rates[0, 0]
    rate_two = rates[1, 0]
    input_weight_first = w_one[0]
    recurrent_weight_first = v_one[0]
    recurrent_weight_second = v_two[0]
    input_weight_second = w_two[0]
    seqs, steps, width_in = inputs.shape
    units = input_weight_first.shape[0]
    position = jnp.arange(steps, dtype=jnp.int32)[None, :]
    valid_rows = (
        (step_mask == 1) & (position >= washout[:, None]) & (position < lengths[:, None])
    ).astype(jnp.float32)
    valid_tm = jnp.transpose(valid_rows, (1, 0))
    series = jnp.transpose(inputs, (1, 0, 2))

    def advance(carry, current_input):
        h_one, h_two, leaky_state_first, leaky_state_second = carry
        preactivation_first = jnp.dot(
            leaky_state_first, input_weight_first, preferred_element_type=jnp.float32
        ) + jnp.dot(current_input, recurrent_weight_first, preferred_element_type=jnp.float32)
        h_one = (1.0 - rate_one) * h_one + rate_one * jnp.tanh(preactivation_first)
        leaky_state_first = h_one.astype(jnp.bfloat16)
        preactivation_second = jnp.dot(
            leaky_state_second, input_weight_second, preferred_element_type=jnp.float32
        ) + jnp.dot(leaky_state_first, recurrent_weight_second, preferred_element_type=jnp.float32)
        h_two = (1.0 - rate_two) * h_two + rate_two * jnp.tanh(preactivation_second)
        leaky_state_second = h_two.astype(jnp.bfloat16)
        return (
            (h_one, h_two, leaky_state_first, leaky_state_second),
            (preactivation_first, preactivation_second, leaky_state_first, leaky_state_second),
        )

    zero_float = jnp.zeros((seqs, units), jnp.float32)
    zero_low = jnp.zeros((seqs, units), jnp.bfloat16)
    final, kept = lax.scan(advance, (zero_float, zero_float, zero_low, zero_low), series)
    preactivation_first, preactivation_second, low_one, low_two = kept
    narrow_count = lax.axis_size("narrow")
    piece = steps // narrow_count
    member = lax.axis_index("narrow")
    dy_tm = jnp.transpose(cotangent, (1, 0, 2))
    dy_tm = jnp.where(valid_tm[:, :, None] > 0, dy_tm, jnp.zeros_like(dy_tm))
    feats = lax.all_to_all(low_two, "narrow", split_axis=0, concat_axis=2, tiled=True)
    head = lax.all_gather(w_out, "narrow", axis=0, tiled=True)
    valid_part = lax.dynamic_slice_in_dim(valid_tm, member * piece, piece, 0)
    dy_part = lax.dynamic_slice_in_dim(dy_tm, member * piece, piece, 0)
    values = feats.astype(jnp.float32)
    totals = lax.psum(statistics(values, valid_part), ("narrow", "wide"))
    mean, inv, normed = normalize(values, totals)
    out_tm = jnp.dot(normed, head, preferred_element_type=jnp.float32) + b_out
    grads = jnp.einsum("pbo,fo->pbf", dy_part, head, preferred_element_type=jnp.float32)
    sum_g = jnp.sum(grads, axis=(0, 1))
    sum_gx = jnp.sum(grads * values, axis=(0, 1))
    head_grad = jnp.einsum("pbf,pbo->fo", normed, dy_part, preferred_element_type=jnp.float32)
    bias_grad = jnp.sum(dy_part.astype(jnp.float32), axis=(0, 1))
    sum_g, sum_gx, head_grad, bias_grad = lax.psum(
        (sum_g, sum_gx, head_grad, bias_grad), ("narrow", "wide")
    )
    dfeat = feature_grad(grads, values, valid_part, mean, inv, totals[2], sum_g, sum_gx)
    dfeat = lax.all_to_all(dfeat, "narrow", split_axis=2, concat_axis=0, tiled=True)
    own_head = lax.dynamic_slice_in_dim(head_grad, member * units, units, 0)
    output = jnp.transpose(out_tm, (1, 0, 2))
    grad_pre_two = back_layer(
        dfeat.astype(jnp.float32), preactivation_second, rate_two, input_weight_second
    )
    upper_cols = lax.all_to_all(grad_pre_two, "wide", split_axis=2, concat_axis=1, tiled=True)
    part_one = lax.all_gather(low_one, "wide", axis=1, tiled=True)
    part_two = lax.all_gather(low_two, "wide", axis=1, tiled=True)
    cols = upper_cols
    sent_vb = outer_sum(part_one, cols)
    sent_wb = outer_sum(shifted(part_two), cols)
    into_one = jnp.einsum(
        "tbq,rq->tbr", grad_pre_two, recurrent_weight_second, preferred_element_type=jnp.float32
    )
    grad_pre_one = back_layer(into_one, preactivation_first, rate_one, input_weight_first)
    input_part = jnp.einsum(
        "tbq,iq->bti", grad_pre_one, recurrent_weight_first, preferred_element_type=jnp.float32
    )
    input_grad = lax.psum(input_part, "narrow")
    lower_cols = lax.all_to_all(grad_pre_one, "wide", split_axis=2, concat_axis=1, tiled=True)
    part_one = lax.all_gather(low_one, "wide", axis=1, tiled=True)
    part_in = lax.all_gather(series, "wide", axis=1, tiled=True)
    cols = lower_cols
    sent_wa = outer_sum(shifted(part_one), cols)
    sent_va = jnp.einsum("tbi,tbq->iq", part_in, cols, preferred_element_type=jnp.float32)
    return (
        output,
        input_grad,
        sent_wa[None],
        sent_va[None],
        sent_vb[None],
        sent_wb[None],
        own_head,
        bias_grad,
    )


def solution(mesh):
    in_specs = (
        P("wide", None, None),
        P("wide", None, None),
        P("wide", None),
        P("wide"),
        P("wide"),
        P(None, "narrow", None),
        P("narrow"),
        P("narrow", None, None),
        P("narrow", None, None),
        P("narrow", None, None),
        P("narrow", None, None),
        P("narrow", None),
        P(),
    )
    out_specs = (
        P("wide", "narrow", None),
        P("wide", None, None),
        P("narrow", None, "wide"),
        P("narrow", None, "wide"),
        P("narrow", None, "wide"),
        P("narrow", None, "wide"),
        P("narrow", None),
        P(),
    )
    return jax.shard_map(
        on_device, mesh=mesh, in_specs=in_specs, out_specs=out_specs, check_vma=False
    )
```

profile of v0, /device:TPU:0, one launch (start us, length us, event | category | flops | bytes accessed | tf_op | source)
XLA Modules:
  0.0 715.1 jit_solution(11959357410567081167)
XLA Ops:
  12.6 94.2 %while.59 = (s32[]{:T(128)}, f32[32,2048]{1,0:T(8,128)S(1)}, f32[32,2048]{1,0:T(8,128)S(1)}, bf16[32,2048]{1,0:T(8,128)(2,1)S(1)}, bf16[32,2048]{1,0:T(8,128)(2,...) while((s32[]{:T(128)}, f32[32,2048]{1,0:T(8,128)S(1)}, ...), condition=%wide.region_1.2_spmd.clone, body=%wide.region_0.1_spmd.clone.sunk | while | flops 819335168 | bytes 80586552 | solution.py:104
  12.6 5.1 fusion.89
  24.3 5.1 fusion.89
  36.1 5.1 fusion.89
  44.8 2.3 bitcast_dynamic-update-slice_fusion.12
  47.9 5.1 fusion.89
  59.7 5.1 fusion.89
  71.4 5.1 fusion.89
  83.2 5.1 fusion.89
  95.0 5.1 fusion.89
  103.6 2.3 bitcast_dynamic-update-slice_fusion.12
  106.8 4.4 all-to-all-start
  111.2 17.2 %all_gather.13 = bf16[8192,10]{0,1:T(8,128)(2,1)S(1)} all-gather(bf16[2048,10]{0,1:T(8,128)(2,1)S(1)} %copy-done.8), channel_id=1, replica_groups=mesh['narrow'=4,'wide'=8] {'narrow'}, dimensions={0}, use_global_device_ids=true | all-gather | bytes 204800 | tf_op jit(solution)/shard_map/all_gather | solution.py:112
  130.7 2.7 copy.72
  133.4 2.7 reshape.67
  136.1 3.5 fusion.29
  141.4 44.6 %all-reduce.10 = (f32[8192]{0:T(1024)S(1)}, f32[]{:T(128)}, f32[8192]{0:T(1024)S(1)}, f32[8192]{0:T(1024)S(1)}, f32[8192]{0:T(1024)S(1)}, /*index=5*/f32[10]{0:T(128)}) all-reduce(f32[8192]{0:T(1024)S(1)} %bitcast.234, f32[]{:T(128)} %get-tuple-element.656, ...), channel_id=1, replica_groups=mesh['narrow'=4,'wide'=8] {'narrow','wide'}, use_global_device_ids=true, to_apply=%region_3.4 | all-reduce | flops 32779 | bytes 262232 | tf_op jit(solution)/shard_map/psum | solution.py:116
  187.4 3.7 add_convert_fusion
  191.0 9.2 %copy.36 = bf16[2,32,8192]{1,0,2:T(2,128)(2,1)} copy(bf16[2,32,8192]{2,1,0:T(8,128)(2,1)} %add_convert_fusion) | data formatting | bytes 2097152 | tf_op jit(solution)/shard_map/convert_element_type | solution.py:11
  200.2 6.4 reshape.80
  206.6 4.2 all-to-all-start.1
  212.8 12.9 %all-to-all-done.1 = bf16[4,2,65536]{2,1,0:T(2,128)(2,1)} async-done(((bf16[4,2,65536]{2,1,0:T(2,128)(2,1)}), bf16[4,2,65536]{2,1,0:T(2,128)(2,1)}, u32[]{:S(2)}, u32[]{:S(2)}) %all-to-all-start.1) | async-done | bytes 1048608 | tf_op jit(solution)/shard_map/all_to_all | solution.py:128
  225.7 5.2 reshape.81
  230.9 6.6 convert_bitcast_fusion
  237.5 11.7 %copy.37 = f32[4,2,32,2048]{3,2,1,0:T(8,128)} copy(f32[4,2,32,2048]{2,1,3,0:T(2,128)} %convert_bitcast_fusion) | data formatting | bytes 4194304 | tf_op jit(solution)/shard_map/convert_element_type | solution.py:132
  250.3 62.2 %while.60 = (s32[]{:T(128)}, f32[32,2048]{1,0:T(8,128)S(1)}, bf16[8,32,2048]{2,1,0:T(8,128)(2,1)}, f32[2048]{0:T(1024)S(1)}, f32[8,32,2048]{2,1,0:T(8,128)}, /*i...) while((s32[]{:T(128)}, f32[32,2048]{1,0:T(8,128)S(1)}, ...), condition=%wide.region_13.14_spmd.clone, body=%wide.region_12.13_spmd.clone.sunk | while | flops 269158400 | bytes 10387604 | solution.py:42
  252.0 6.0 convolution_add_fusion.7
  259.8 6.0 convolution_add_fusion.7
  267.6 6.0 convolution_add_fusion.7
  275.4 6.0 convolution_add_fusion.7
  283.1 6.0 convolution_add_fusion.7
  290.9 6.0 convolution_add_fusion.7
  298.7 6.0 convolution_add_fusion.7
  306.4 6.0 convolution_add_fusion.7
  312.4 7.4 %fusion.17 = f32[8,32,2048]{2,1,0:T(8,128)} fusion(bf16[8,32,2048]{2,1,0:T(8,128)(2,1)} %get-tuple-element.425, bf16[1,2048,2048]{2,1,0:T(8,128)(2,1)} %bitcast.199), kind=kOutput, calls=%fused_computation.39 | convolution fusion | flops 2147483648 | bytes 11534336 | tf_op jit(solution)/shard_map/tbq,rq->tbr/dot_general | solution.py:140
  320.9 62.0 %while.61 = (s32[]{:T(128)}, f32[32,2048]{1,0:T(8,128)S(1)}, bf16[8,32,2048]{2,1,0:T(8,128)(2,1)}, f32[2048]{0:T(1024)S(1)}, f32[8,32,2048]{2,1,0:T(8,128)}, /*i...) while((s32[]{:T(128)}, f32[32,2048]{1,0:T(8,128)S(1)}, ...), condition=%wide.region_15.16_spmd.clone, body=%wide.region_14.15_spmd.clone.sunk | while | flops 269158400 | bytes 10387604 | solution.py:42
  322.7 6.0 convolution_add_fusion.8
  330.4 6.0 convolution_add_fusion.8
  338.2 6.0 convolution_add_fusion.8
  346.0 6.0 convolution_add_fusion.8
  353.7 6.0 convolution_add_fusion.8
  361.5 6.0 convolution_add_fusion.8
  369.2 6.0 convolution_add_fusion.8
  377.0 6.0 convolution_add_fusion.8
  382.9 2.3 convolution_bitcast_fusion.2
  385.3 2.8 copy.38
  388.4 2.8 copy.45
  391.2 4.2 copy.42
  395.5 7.9 %reshape.84 = bf16[8,2,32768]{2,1,0:T(2,128)(2,1)} reshape(bf16[2048,8,32]{2,1,0:T(8,128)(2,1)} %bitcast.204) | data formatting | bytes 2097152
  403.3 4.4 all-to-all-start.3
  407.7 4.3 copy.40
  412.0 7.8 %reshape.82 = bf16[8,2,32768]{2,1,0:T(2,128)(2,1)} reshape(bf16[2048,8,32]{2,1,0:T(8,128)(2,1)} %bitcast.205) | data formatting | bytes 2097152
  419.9 35.7 %all-to-all-done.3 = bf16[8,2,32768]{2,1,0:T(2,128)(2,1)} async-done(((bf16[8,2,32768]{2,1,0:T(2,128)(2,1)}), bf16[8,2,32768]{2,1,0:T(2,128)(2,1)}, u32[]{:S(2)}, u32[]{:S(2)}) %all-to-all-start.3) | async-done | bytes 1048608 | tf_op jit(solution)/shard_map/all_to_all | solution.py:134
  455.6 3.6 all-to-all-start.2
  459.1 83.5 %all_gather.15 = bf16[8,256,100]{2,1,0:T(8,128)(2,1)} all-gather(bf16[8,32,100]{2,1,0:T(8,128)(2,1)S(1)} %get-tuple-element.1043), channel_id=1, replica_groups=mesh['narrow'=4,'wide'=8] {'wide'}, dimensions={1}, use_global_device_ids=true | all-gather | bytes 460800 | tf_op jit(solution)/shard_map/all_gather | solution.py:150
  547.3 7.1 reshape.85
  554.3 5.5 copy.52
  559.9 5.3 copy.43
  565.2 4.6 reshape.83
  569.7 4.5 copy.41
  575.3 19.8 %fusion.23 = f32[1,2048,256]{2,1,0:T(8,128)} fusion(bf16[8,256,256]{2,1,0:T(8,128)(2,1)S(1)} %bitcast.212, bf16[7,256,2048]{2,0,1:T(8,128)(2,1)} %bitcast.239), kind=kOutput, calls=%fused_computation.47 | convolution fusion | flops 1879048192 | bytes 10485760 | tf_op jit(solution)/shard_map/tbr,tbq->rq/dot_general | solution.py:51
  595.1 87.9 %all-gather.5.cloned.1.call-done = bf16[8,256,2048]{2,0,1:T(8,128)(2,1)} async-done(((bf16[8,32,2048]{2,0,1:T(8,128)(2,1)}), bf16[8,256,2048]{2,0,1:T(8,128)(2,1)}) %all-gather.5.cloned.1.call-update) | async-done | bytes 8388624 | tf_op jit(solution)/shard_map/all_gather | solution.py:136
  683.1 19.7 %fusion.26 = f32[1,2048,256]{2,1,0:T(8,128)} fusion(bf16[8,256,256]{2,1,0:T(8,128)(2,1)S(1)} %bitcast.230, bf16[7,256,2048]{2,0,1:T(8,128)(2,1)} %bitcast.240), kind=kOutput, calls=%fused_computation.48 | convolution fusion | flops 1879048192 | bytes 10485760 | tf_op jit(solution)/shard_map/tbr,tbq->rq/dot_general | solution.py:51
  702.8 4.7 convolution_bitcast_fusion.1
  (234 shorter events, 96.6 us)
Async XLA Ops:
  8.0 4.6 copy-start.1
  12.6 6.0 slice-start
  12.6 6.0 slice-start.1
  17.7 2.5 slice-start.2
  18.6 2.7 slice-start.3
  24.3 6.0 slice-start
  24.3 6.0 slice-start.1
  29.4 2.5 slice-start.2
  30.3 2.7 slice-start.3
  36.1 6.0 slice-start
  36.1 6.0 slice-start.1
  41.2 2.5 slice-start.2
  42.1 2.7 slice-start.3
  47.9 6.0 slice-start
  47.9 6.0 slice-start.1
  53.0 2.5 slice-start.2
  53.9 2.7 slice-start.3
  59.7 6.0 slice-start
  59.7 6.0 slice-start.1
  64.7 2.5 slice-start.2
  65.7 2.7 slice-start.3
  71.4 6.0 slice-start
  71.4 6.0 slice-start.1
  76.5 2.5 slice-start.2
  77.4 2.7 slice-start.3
  83.2 6.0 slice-start
  83.2 6.0 slice-start.1
  88.3 2.5 slice-start.2
  89.2 2.7 slice-start.3
  95.0 6.0 slice-start
  95.0 6.0 slice-start.1
  100.0 2.5 slice-start.2
  101.0 2.7 slice-start.3
  106.7 4.4 copy-start.9
  106.7 4.5 copy-start.8
  106.7 21.7 %copy-start.10 = (s32[32,8]{0,1:T(8,128)S(1)}, s32[32,8]{0,1:T(8,128)}, u32[]{:S(2)}) copy-start(s32[32,8]{0,1:T(8,128)} %param.21) | copy-start | bytes 3076
  106.7 21.7 %copy-start.11 = (s32[32]{0:T(128)S(1)}, s32[32]{0:T(128)}, u32[]{:S(2)}) copy-start(s32[32]{0:T(128)} %param.23) | copy-start | bytes 388
  106.8 21.7 %copy-start.12 = (s32[32]{0:T(128)S(1)}, s32[32]{0:T(128)}, u32[]{:S(2)}) copy-start(s32[32]{0:T(128)} %param.22) | copy-start | bytes 388
  106.8 22.5 %all-to-all-start = ((bf16[8,32,2048]{2,1,0:T(8,128)(2,1)}), bf16[8,32,2048]{2,1,0:T(8,128)(2,1)}, u32[]{:S(2)}, u32[]{:S(2)}) async-start(bf16[8,32,2048]{2,1,0:T(8,128)(2,1)} %get-tuple-element.423), calls=%async_computation | async-start | bytes 2097152 | tf_op jit(solution)/shard_map/all_to_all | solution.py:111
  111.2 28.4 %copy-start.7 = (bf16[32,8,10]{0,2,1:T(8,128)(2,1)}, bf16[32,8,10]{0,2,1:T(8,128)(2,1)S(1)}, u32[]{:S(2)}) copy-start(bf16[32,8,10]{0,2,1:T(8,128)(2,1)S(1)} %copy.74) | copy-start | bytes 15364
  130.7 2.7 copy-start
  206.6 19.1 %all-to-all-start.1 = ((bf16[4,2,65536]{2,1,0:T(2,128)(2,1)}), bf16[4,2,65536]{2,1,0:T(2,128)(2,1)}, u32[]{:S(2)}, u32[]{:S(2)}) async-start(bf16[4,2,65536]{2,1,0:T(2,128)(2,1)} %reshape.80), calls=%async_computation.1 | async-start | bytes 2097152 | tf_op jit(solution)/shard_map/all_to_all | solution.py:128
  210.8 333.2 %all-reduce.9.cloned.1.call-start = ((), (), s32[]{:S(2)}) async-start(), calls=%async_computation.7 | async-start | bytes 1048576 | tf_op jit(solution)/shard_map/psum | solution.py:124
  212.8 332.9 %all-reduce.7.cloned.1.call-start = ((), (), s32[]{:S(2)}) async-start(), calls=%async_computation.4 | async-start | bytes 262144 | tf_op jit(solution)/shard_map/psum | solution.py:147
  385.3 190.0 %all-gather.3.cloned.1.call-start = ((), (), s32[]{:S(2)}) async-start(), calls=%async_computation.5 | async-start | bytes 9437184 | tf_op jit(solution)/shard_map/all_gather | solution.py:149
  388.1 3.1 copy-start.3
  388.1 295.0 %all-gather.5.cloned.1.call-start = ((), (), s32[]{:S(2)}) async-start(), calls=%async_computation.6 | async-start | bytes 9437184 | tf_op jit(solution)/shard_map/all_gather | solution.py:136
  403.3 4.4 copy-start.2
  403.3 52.2 %all-to-all-start.3 = ((bf16[8,2,32768]{2,1,0:T(2,128)(2,1)}), bf16[8,2,32768]{2,1,0:T(2,128)(2,1)}, u32[]{:S(2)}, u32[]{:S(2)}) async-start(bf16[8,2,32768]{2,1,0:T(2,128)(2,1)} %reshape.84), calls=%async_computation.3 | async-start | bytes 2097152 | tf_op jit(solution)/shard_map/all_to_all | solution.py:134
  419.9 122.8 %copy-start.13 = (f32[10]{0:T(128)S(1)}, f32[10]{0:T(128)}, u32[]{:S(2)}) copy-start(f32[10]{0:T(128)} %param.31) | copy-start | bytes 124
  455.6 109.6 %all-to-all-start.2 = ((bf16[8,2,32768]{2,1,0:T(2,128)(2,1)}), bf16[8,2,32768]{2,1,0:T(2,128)(2,1)S(1)}, u32[]{:S(2)}, u32[]{:S(2)}) async-start(bf16[8,2,32768]{2,1,0:T(2,128)(2,1)} %reshape.82), calls=%async_computation.2 | async-start | bytes 2097152 | tf_op jit(solution)/shard_map/all_to_all | solution.py:148
  569.7 4.5 copy-start.4
  575.3 107.8 %copy-start.6 = (bf16[8,32,8,256]{3,1,2,0:T(8,128)(2,1)S(1)}, bf16[8,32,8,256]{3,1,2,0:T(8,128)(2,1)}, u32[]{:S(2)}) copy-start(bf16[8,32,8,256]{3,1,2,0:T(8,128)(2,1)} %copy.43) | copy-start | bytes 3145732
  683.1 19.7 %copy-start.5 = (bf16[8,32,8,256]{3,0,1,2:T(8,128)(2,1)S(1)}, bf16[8,32,8,256]{3,0,1,2:T(8,128)(2,1)}, u32[]{:S(2)}) copy-start(bf16[8,32,8,256]{3,0,1,2:T(8,128)(2,1)} %copy.52) | copy-start | bytes 3145732
  683.1 19.7 %copy-start.14 = (bf16[8,256,2048]{2,0,1:T(8,128)(2,1)S(1)}, bf16[8,256,2048]{2,0,1:T(8,128)(2,1)}, u32[]{:S(2)}) copy-start(bf16[8,256,2048]{2,0,1:T(8,128)(2,1)} %all-gather.3.cloned.1.call-done) | copy-start | bytes 25165828
Sparse Core Ops, SparseCore 0:
  216.9 127.4 all-reduce.8
  385.4 29.5 all-reduce.6
Sparse Core Ops, SparseCore 1:
  388.5 169.6 all-gather.2
  560.1 123.0 all-gather.4
where the time goes:
time: 725 us; the launch traced here: 715 us
  matrix products  233 us (32%)
  blocking collectives  145 us (20%)
  waiting for transfers between devices  137 us (19%)
  local copies, waits for them, and re-layouts  120 us (17%)
  other arithmetic  46.4 us (6%)
  starting transfers between devices  16.9 us (2%)
  between operations  16.7 us (2%)
    dot_general x16, matrix products, back_step(): lax.dot_general(grad_p, weight, (((1,), (1,)), ((), ())), preferred_eleme...  95.6 us
    all_gather x1, waiting for transfers between devices, on_device(): part_two = lax.all_gather(low_two, 'wide', axis=1, tiled=True)  87.9 us
    all_gather x1, blocking collectives, on_device(): part_in = lax.all_gather(series, 'wide', axis=1, tiled=True)  83.5 us
    psum x1, blocking collectives, on_device(): totals = lax.psum(statistics(values, valid_part), ('narrow', 'wide'))  44.6 us
    dot_general x3, matrix products, outer_sum(): jnp.einsum('tbr,tbq->rq', left, right, preferred_element_type=jnp.float32)  44.3 us
    unnamed x43, local copies, waits for them, and re-layouts  42.8 us
    dot_general x8, matrix products, advance(): jnp.dot(leaky_state_first, input_weight_first, preferred_element_type=jnp...  40.6 us
    all_to_all x1, waiting for transfers between devices, on_device(): lax.all_to_all(grad_pre_two, 'wide', split_axis=2, concat_axis=1, tiled=T...  35.7 us
  transfers between devices with their start and end apart: 8, of which 3 were waited for; matrix products, arithmetic and copies ran while one was open for 34% of the time, Pallas kernels for 0%

commit v1 on v0

--- a/solution.py
+++ b/solution.py
@@ -113,7 +113,7 @@
     valid_part = lax.dynamic_slice_in_dim(valid_tm, member * piece, piece, 0)
     dy_part = lax.dynamic_slice_in_dim(dy_tm, member * piece, piece, 0)
     values = feats.astype(jnp.float32)
-    totals = lax.psum(statistics(values, valid_part), ("narrow", "wide"))
+    totals = lax.psum(lax.psum(statistics(values, valid_part), "wide"), "narrow")
     mean, inv, normed = normalize(values, totals)
     out_tm = jnp.dot(normed, head, preferred_element_type=jnp.float32) + b_out
     grads = jnp.einsum("pbo,fo->pbf", dy_part, head, preferred_element_type=jnp.float32)

time: 725 us -> 806 us (1.11)
  waiting for transfers between devices: 137 us -> 197 us
  local copies, waits for them, and re-layouts: 120 us -> 130 us
    psum x1 -> x2, waiting for transfers between devices: 0.01 us -> 67.6 us  [on_device(): lax.psum((sum_g, sum_gx, head_grad, bias_grad), ('narrow', 'wide'))]
    all_to_all x1, local copies, waits for them, and re-layouts: 4.47 us -> 13.2 us  [on_device(): lax.all_to_all(grad_pre_one, 'wide', split_axis=2, concat_axis=1, tiled=T...]
    all_gather x1, waiting for transfers between devices: 87.9 us -> 79.5 us  [on_device(): part_two = lax.all_gather(low_two, 'wide', axis=1, tiled=True)]
    psum x1 -> x2, blocking collectives: 44.6 us -> 52.7 us  [the longest x1 40.2 us: on_device(): lax.psum(statistics(values, valid_part), 'wide')]
    unnamed x43 -> x46, local copies, waits for them, and re-layouts: 42.8 us -> 43.5 us
  transfers between devices with their start and end apart: 8 -> 9, of which waited for: 3 -> 4; matrix products, arithmetic and copies ran while one was open for 34% -> 32% of each run, Pallas kernels for 0% -> 0%
where the time goes in v1:
time: 806 us; the launch traced here: 795 us
  matrix products  233 us (29%)
  waiting for transfers between devices  197 us (24%)
  blocking collectives  153 us (19%)
  local copies, waits for them, and re-layouts  130 us (16%)
  other arithmetic  48.4 us (6%)
  starting transfers between devices  17.8 us (2%)
  between operations  16.6 us (2%)
    dot_general x16, matrix products, back_step(): lax.dot_general(grad_p, weight, (((1,), (1,)), ((), ())), preferred_eleme...  95.5 us
    all_gather x1, blocking collectives, on_device(): part_in = lax.all_gather(series, 'wide', axis=1, tiled=True)  83.1 us
    all_gather x1, waiting for transfers between devices, on_device(): part_two = lax.all_gather(low_two, 'wide', axis=1, tiled=True)  79.5 us
    psum x2, waiting for transfers between devices, on_device(): lax.psum((sum_g, sum_gx, head_grad, bias_grad), ('narrow', 'wide'))  67.6 us
    dot_general x3, matrix products, outer_sum(): jnp.einsum('tbr,tbq->rq', left, right, preferred_element_type=jnp.float32)  44.1 us
    unnamed x46, local copies, waits for them, and re-layouts  43.5 us
    dot_general x8, matrix products, advance(): jnp.dot(leaky_state_first, input_weight_first, preferred_element_type=jnp...  40.6 us
    psum x1, blocking collectives, on_device(): lax.psum(statistics(values, valid_part), 'wide')  40.2 us
  transfers between devices with their start and end apart: 9, of which 4 were waited for; matrix products, arithmetic and copies ran while one was open for 32% of the time, Pallas kernels for 0%

profile of v1, /device:TPU:0, one launch (start us, length us, event | category | flops | bytes accessed | tf_op | source)
XLA Modules:
  0.0 795.3 jit_solution(13583776006990727544)
XLA Ops:
  12.6 94.1 %while.59 = (s32[]{:T(128)}, f32[32,2048]{1,0:T(8,128)S(1)}, f32[32,2048]{1,0:T(8,128)S(1)}, bf16[32,2048]{1,0:T(8,128)(2,1)S(1)}, bf16[32,2048]{1,0:T(8,128)(2,...) while((s32[]{:T(128)}, f32[32,2048]{1,0:T(8,128)S(1)}, ...), condition=%wide.region_1.2_spmd.clone, body=%wide.region_0.1_spmd.clone.sunk | while | flops 819335168 | bytes 80586552 | solution.py:104
  12.6 5.1 fusion.89
  24.3 5.1 fusion.89
  36.1 5.1 fusion.89
  47.8 5.1 fusion.89
  59.6 5.1 fusion.89
  71.4 5.1 fusion.89
  83.2 5.1 fusion.89
  94.9 5.1 fusion.89
  106.7 4.4 all-to-all-start
  111.2 17.2 %all_gather.13 = bf16[8192,10]{0,1:T(8,128)(2,1)S(1)} all-gather(bf16[2048,10]{0,1:T(8,128)(2,1)S(1)} %copy-done.8), channel_id=1, replica_groups=mesh['narrow'=4,'wide'=8] {'narrow'}, dimensions={0}, use_global_device_ids=true | all-gather | bytes 204800 | tf_op jit(solution)/shard_map/all_gather | solution.py:112
  131.2 2.7 copy.72
  133.8 2.7 reshape.67
  136.5 3.5 fusion.29
  140.1 2.4 fusion.45
  142.5 40.2 %all-reduce.16 = (f32[8192]{0:T(1024)S(1)}, f32[]{:T(128)}, f32[8192]{0:T(1024)S(1)}) all-reduce(f32[8192]{0:T(1024)S(1)} %bitcast.234, f32[]{:T(128)} %get-tuple-element.659, f32[8192]{0:T(1024)S(1)} %bitcast.235), channel_id=1, replica_groups=mesh['narrow'=4,'wide'=8] {'wide'}, use_global_device_ids=true, to_apply=%region_3.4 | all-reduce | flops 16385 | bytes 131080 | tf_op jit(solution)/shard_map/psum | solution.py:116
  182.7 12.5 %all-reduce.17 = (f32[8192]{0:T(1024)S(1)}, f32[]{:T(128)}, f32[8192]{0:T(1024)S(1)}) all-reduce(f32[8192]{0:T(1024)S(1)} %get-tuple-element.631, f32[]{:T(128)} %get-tuple-element.632, f32[8192]{0:T(1024)S(1)} %get-tuple-element.633), channel_id=1, replica_groups=mesh['narrow'=4,'wide'=8] {'narrow'}, use_global_device_ids=true, to_apply=%region_4.5 | all-reduce | flops 16385 | bytes 131080 | tf_op jit(solution)/shard_map/psum | solution.py:116
  195.2 67.6 %all-reduce.15.cloned.1.call-done = (f32[8192]{0:T(1024)}, f32[8192]{0:T(1024)}, f32[10]{0:T(128)}) async-done(((f32[8192]{0:T(1024)}, f32[8192]{0:T(1024)}, f32[10]{0:T(128)}), (f32[8192]{0:T(1024)}, f32[8192]{0:T(1024)}, f32[10]{0:T(128)})) %all-reduce.15.cloned.1.call-update) | async-done | bytes 65592 | tf_op jit(solution)/shard_map/psum | solution.py:124
  265.6 3.7 add_convert_fusion
  269.3 9.2 %copy.36 = bf16[2,32,8192]{1,0,2:T(2,128)(2,1)} copy(bf16[2,32,8192]{2,1,0:T(8,128)(2,1)} %add_convert_fusion) | data formatting | bytes 2097152 | tf_op jit(solution)/shard_map/convert_element_type | solution.py:11
  278.5 6.4 reshape.80
  284.9 4.2 all-to-all-start.1
  291.1 12.9 %all-to-all-done.1 = bf16[4,2,65536]{2,1,0:T(2,128)(2,1)} async-done(((bf16[4,2,65536]{2,1,0:T(2,128)(2,1)}), bf16[4,2,65536]{2,1,0:T(2,128)(2,1)}, u32[]{:S(2)}, u32[]{:S(2)}) %all-to-all-start.1) | async-done | bytes 1048608 | tf_op jit(solution)/shard_map/all_to_all | solution.py:128
  304.0 5.2 reshape.81
  309.2 6.6 convert_bitcast_fusion
  315.8 11.7 %copy.37 = f32[4,2,32,2048]{3,2,1,0:T(8,128)} copy(f32[4,2,32,2048]{2,1,3,0:T(2,128)} %convert_bitcast_fusion) | data formatting | bytes 4194304 | tf_op jit(solution)/shard_map/convert_element_type | solution.py:132
  328.6 62.1 %while.60 = (s32[]{:T(128)}, f32[32,2048]{1,0:T(8,128)S(1)}, bf16[8,32,2048]{2,1,0:T(8,128)(2,1)}, f32[2048]{0:T(1024)S(1)}, f32[8,32,2048]{2,1,0:T(8,128)}, /*i...) while((s32[]{:T(128)}, f32[32,2048]{1,0:T(8,128)S(1)}, ...), condition=%wide.region_16.17_spmd.clone, body=%wide.region_15.16_spmd.clone.sunk | while | flops 269158400 | bytes 10387604 | solution.py:42
  330.3 6.0 convolution_add_fusion.7
  338.1 6.0 convolution_add_fusion.7
  345.9 6.0 convolution_add_fusion.7
  353.6 6.0 convolution_add_fusion.7
  361.4 6.0 convolution_add_fusion.7
  369.2 6.0 convolution_add_fusion.7
  376.9 6.0 convolution_add_fusion.7
  384.7 6.0 convolution_add_fusion.7
  390.7 7.4 fusion.17
  399.2 62.0 %while.61 = (s32[]{:T(128)}, f32[32,2048]{1,0:T(8,128)S(1)}, bf16[8,32,2048]{2,1,0:T(8,128)(2,1)}, f32[2048]{0:T(1024)S(1)}, f32[8,32,2048]{2,1,0:T(8,128)}, /*i...) while((s32[]{:T(128)}, f32[32,2048]{1,0:T(8,128)S(1)}, ...), condition=%wide.region_18.19_spmd.clone, body=%wide.region_17.18_spmd.clone.sunk | while | flops 269158400 | bytes 10387604 | solution.py:42
  400.9 6.0 convolution_add_fusion.8
  408.7 6.0 convolution_add_fusion.8
  416.5 6.0 convolution_add_fusion.8
  424.3 6.0 convolution_add_fusion.8
  432.0 6.0 convolution_add_fusion.8
  439.8 6.0 convolution_add_fusion.8
  447.5 6.0 convolution_add_fusion.8
  455.2 6.0 convolution_add_fusion.8
  463.6 2.8 copy.38
  466.5 2.8 copy.45
  469.3 4.2 copy.42
  473.6 8.0 %reshape.84 = bf16[8,2,32768]{2,1,0:T(2,128)(2,1)} reshape(bf16[2048,8,32]{2,1,0:T(8,128)(2,1)} %bitcast.204) | data formatting | bytes 2097152
  481.5 5.4 all-to-all-start.3
  486.9 4.3 copy.40
  491.2 7.8 reshape.82
  499.1 36.5 %all-to-all-done.3 = bf16[8,2,32768]{2,1,0:T(2,128)(2,1)} async-done(((bf16[8,2,32768]{2,1,0:T(2,128)(2,1)}), bf16[8,2,32768]{2,1,0:T(2,128)(2,1)}, u32[]{:S(2)}, u32[]{:S(2)}) %all-to-all-start.3) | async-done | bytes 1048608 | tf_op jit(solution)/shard_map/all_to_all | solution.py:134
  535.5 3.6 all-to-all-start.2
  539.1 83.1 %all_gather.15 = bf16[8,256,100]{2,1,0:T(8,128)(2,1)} all-gather(bf16[8,32,100]{2,1,0:T(8,128)(2,1)S(1)} %get-tuple-element.1060), channel_id=1, replica_groups=mesh['narrow'=4,'wide'=8] {'wide'}, dimensions={1}, use_global_device_ids=true | all-gather | bytes 460800 | tf_op jit(solution)/shard_map/all_gather | solution.py:150
  626.8 7.1 reshape.85
  633.9 5.5 copy.52
  639.4 5.3 copy.43
  644.7 4.6 reshape.83
  649.3 13.2 %copy.41 = bf16[8,32,8,256]{3,1,2,0:T(8,128)(2,1)S(1)} copy(bf16[8,32,8,256]{1,0,3,2:T(8,128)(2,1)} %bitcast.206) | data formatting | bytes 2097152 | tf_op jit(solution)/shard_map/all_to_all | solution.py:148
  663.6 19.6 %fusion.23 = f32[1,2048,256]{2,1,0:T(8,128)} fusion(bf16[8,256,256]{2,1,0:T(8,128)(2,1)S(1)} %bitcast.212, bf16[7,256,2048]{2,0,1:T(8,128)(2,1)} %bitcast.239), kind=kOutput, calls=%fused_computation.47 | convolution fusion | flops 1879048192 | bytes 10485760 | tf_op jit(solution)/shard_map/tbr,tbq->rq/dot_general | solution.py:51
  683.2 79.5 %all-gather.5.cloned.1.call-done = bf16[8,256,2048]{2,0,1:T(8,128)(2,1)} async-done(((bf16[8,32,2048]{2,0,1:T(8,128)(2,1)}), bf16[8,256,2048]{2,0,1:T(8,128)(2,1)}) %all-gather.5.cloned.1.call-update) | async-done | bytes 8388624 | tf_op jit(solution)/shard_map/all_gather | solution.py:136
  762.8 19.8 %fusion.26 = f32[1,2048,256]{2,1,0:T(8,128)} fusion(bf16[8,256,256]{2,1,0:T(8,128)(2,1)S(1)} %bitcast.230, bf16[7,256,2048]{2,0,1:T(8,128)(2,1)} %bitcast.240), kind=kOutput, calls=%fused_computation.48 | convolution fusion | flops 1879048192 | bytes 10485760 | tf_op jit(solution)/shard_map/tbr,tbq->rq/dot_general | solution.py:51
  782.6 4.7 convolution_bitcast_fusion.1
  (241 shorter events, 104.0 us)
Async XLA Ops:
  8.0 4.6 copy-start.1
  12.6 6.0 slice-start
  12.6 6.0 slice-start.1
  17.6 2.5 slice-start.2
  18.6 2.7 slice-start.3
  24.3 6.0 slice-start
  24.3 6.0 slice-start.1
  29.4 2.5 slice-start.2
  30.3 2.7 slice-start.3
  36.1 6.0 slice-start
  36.1 6.0 slice-start.1
  41.2 2.5 slice-start.2
  42.1 2.7 slice-start.3
  47.8 6.0 slice-start
  47.8 6.0 slice-start.1
  52.9 2.5 slice-start.2
  53.8 2.7 slice-start.3
  59.6 6.0 slice-start
  59.6 6.0 slice-start.1
  64.7 2.5 slice-start.2
  65.6 2.7 slice-start.3
  71.4 6.0 slice-start
  71.4 6.0 slice-start.1
  76.5 2.5 slice-start.2
  77.4 2.7 slice-start.3
  83.1 6.0 slice-start
  83.2 6.0 slice-start.1
  88.2 2.5 slice-start.2
  89.1 2.7 slice-start.3
  94.9 6.0 slice-start
  94.9 6.0 slice-start.1
  100.0 2.5 slice-start.2
  100.9 2.7 slice-start.3
  106.7 4.5 copy-start.9
  106.7 4.5 copy-start.8
  106.7 21.7 %copy-start.10 = (s32[32,8]{0,1:T(8,128)S(1)}, s32[32,8]{0,1:T(8,128)}, u32[]{:S(2)}) copy-start(s32[32,8]{0,1:T(8,128)} %param.21) | copy-start | bytes 3076
  106.7 21.7 %copy-start.11 = (s32[32]{0:T(128)S(1)}, s32[32]{0:T(128)}, u32[]{:S(2)}) copy-start(s32[32]{0:T(128)} %param.23) | copy-start | bytes 388
  106.7 21.7 %copy-start.12 = (s32[32]{0:T(128)S(1)}, s32[32]{0:T(128)}, u32[]{:S(2)}) copy-start(s32[32]{0:T(128)} %param.22) | copy-start | bytes 388
  106.7 23.0 %all-to-all-start = ((bf16[8,32,2048]{2,1,0:T(8,128)(2,1)}), bf16[8,32,2048]{2,1,0:T(8,128)(2,1)}, u32[]{:S(2)}, u32[]{:S(2)}) async-start(bf16[8,32,2048]{2,1,0:T(8,128)(2,1)} %get-tuple-element.423), calls=%async_computation | async-start | bytes 2097152 | tf_op jit(solution)/shard_map/all_to_all | solution.py:111
  111.1 151.6 %all-reduce.15.cloned.1.call-start = ((), (), s32[]{:S(2)}) async-start(), calls=%async_computation.8 | async-start | bytes 132096 | tf_op jit(solution)/shard_map/psum | solution.py:124
  111.2 28.9 %copy-start.7 = (bf16[32,8,10]{0,2,1:T(8,128)(2,1)}, bf16[32,8,10]{0,2,1:T(8,128)(2,1)S(1)}, u32[]{:S(2)}) copy-start(bf16[32,8,10]{0,2,1:T(8,128)(2,1)S(1)} %copy.74) | copy-start | bytes 15364
  131.1 2.7 copy-start
  284.9 19.1 %all-to-all-start.1 = ((bf16[4,2,65536]{2,1,0:T(2,128)(2,1)}), bf16[4,2,65536]{2,1,0:T(2,128)(2,1)}, u32[]{:S(2)}, u32[]{:S(2)}) async-start(bf16[4,2,65536]{2,1,0:T(2,128)(2,1)} %reshape.80), calls=%async_computation.1 | async-start | bytes 2097152 | tf_op jit(solution)/shard_map/all_to_all | solution.py:128
  289.1 334.5 %all-reduce.13.cloned.1.call-start = ((), (), s32[]{:S(2)}) async-start(), calls=%async_computation.7 | async-start | bytes 1048576 | tf_op jit(solution)/shard_map/psum | solution.py:124
  291.1 334.1 %all-reduce.11.cloned.1.call-start = ((), (), s32[]{:S(2)}) async-start(), calls=%async_computation.4 | async-start | bytes 262144 | tf_op jit(solution)/shard_map/psum | solution.py:147
  463.6 200.0 %all-gather.3.cloned.1.call-start = ((), (), s32[]{:S(2)}) async-start(), calls=%async_computation.5 | async-start | bytes 9437184 | tf_op jit(solution)/shard_map/all_gather | solution.py:149
  466.4 2.9 copy-start.3
  466.4 296.3 %all-gather.5.cloned.1.call-start = ((), (), s32[]{:S(2)}) async-start(), calls=%async_computation.6 | async-start | bytes 9437184 | tf_op jit(solution)/shard_map/all_gather | solution.py:136
  481.5 5.4 copy-start.2
  481.5 54.0 %all-to-all-start.3 = ((bf16[8,2,32768]{2,1,0:T(2,128)(2,1)}), bf16[8,2,32768]{2,1,0:T(2,128)(2,1)}, u32[]{:S(2)}, u32[]{:S(2)}) async-start(bf16[8,2,32768]{2,1,0:T(2,128)(2,1)} %reshape.84), calls=%async_computation.3 | async-start | bytes 2097152 | tf_op jit(solution)/shard_map/all_to_all | solution.py:134
  499.1 123.2 %copy-start.13 = (f32[10]{0:T(128)S(1)}, f32[10]{0:T(128)}, u32[]{:S(2)}) copy-start(f32[10]{0:T(128)} %param.31) | copy-start | bytes 124
  535.5 109.2 %all-to-all-start.2 = ((bf16[8,2,32768]{2,1,0:T(2,128)(2,1)}), bf16[8,2,32768]{2,1,0:T(2,128)(2,1)S(1)}, u32[]{:S(2)}, u32[]{:S(2)}) async-start(bf16[8,2,32768]{2,1,0:T(2,128)(2,1)} %reshape.82), calls=%async_computation.2 | async-start | bytes 2097152 | tf_op jit(solution)/shard_map/all_to_all | solution.py:148
  649.3 13.2 %copy-start.4 = (bf16[8,256,100]{2,1,0:T(8,128)(2,1)S(1)}, bf16[8,256,100]{2,1,0:T(8,128)(2,1)}, u32[]{:S(2)}) copy-start(bf16[8,256,100]{2,1,0:T(8,128)(2,1)} %all_gather.15) | copy-start | bytes 1228804
  663.6 99.2 %copy-start.6 = (bf16[8,32,8,256]{3,1,2,0:T(8,128)(2,1)S(1)}, bf16[8,32,8,256]{3,1,2,0:T(8,128)(2,1)}, u32[]{:S(2)}) copy-start(bf16[8,32,8,256]{3,1,2,0:T(8,128)(2,1)} %copy.43) | copy-start | bytes 3145732
  762.8 19.8 %copy-start.5 = (bf16[8,32,8,256]{3,0,1,2:T(8,128)(2,1)S(1)}, bf16[8,32,8,256]{3,0,1,2:T(8,128)(2,1)}, u32[]{:S(2)}) copy-start(bf16[8,32,8,256]{3,0,1,2:T(8,128)(2,1)} %copy.52) | copy-start | bytes 3145732
  762.8 19.8 %copy-start.14 = (bf16[8,256,2048]{2,0,1:T(8,128)(2,1)S(1)}, bf16[8,256,2048]{2,0,1:T(8,128)(2,1)}, u32[]{:S(2)}) copy-start(bf16[8,256,2048]{2,0,1:T(8,128)(2,1)} %all-gather.3.cloned.1.call-done) | copy-start | bytes 25165828
  782.6 4.7 copy-start.15
Sparse Core Ops, SparseCore 0:
  142.6 120.0 all-reduce.14
  295.2 129.0 all-reduce.12
  463.7 31.2 all-reduce.10
Sparse Core Ops, SparseCore 1:
  466.7 170.6 all-gather.2
  639.4 123.3 all-gather.4
